TPU v7x, 32 devices: a whole 2x2x4 slice. The times are simulated.
32 devices in a mesh: parts: 2 (over y), blk: 8 (over z, x), ugrp: 2 (over core).
Axes of the slice: x: 2, y: 2, z: 4, core: 2. Of those that a mesh axis runs over, the one named last changes fastest.
Arguments:
- rating_tiles: bfloat16 [32768, 4, 256], P(('parts', 'blk', 'ugrp')), parts along dimension 0, may hold values from -6 to 6
- tile_mask: int32 [32768, 4, 256], P(('parts', 'blk', 'ugrp')), parts along dimension 0, may hold values 0 or 1
- user_rows: float32 [32768, 256], P(('parts', 'blk', 'ugrp')), parts along dimension 0, may hold values from -1.5 to 1.5
- item_rows: float32 [4096, 256], P(('parts', 'blk', 'ugrp')), parts along dimension 0, may hold values from -1.5 to 1.5
- user_noise: bfloat16 [2, 32768, 256], P(None, ('parts', 'blk', 'ugrp')), parts along dimension 1, may hold values from -6 to 6
- item_noise: bfloat16 [2, 4096, 256], P(None, ('parts', 'blk', 'ugrp')), parts along dimension 1, may hold values from -6 to 6
Outputs:
- new_users: float32 [32768, 256], P(('parts', 'blk', 'ugrp')), parts along dimension 0
- new_items: float32 [4096, 256], P(('parts', 'blk', 'ugrp')), parts along dimension 0
There are 2 independent parts, one for each index of `parts`. A program takes and returns all parts, laid end to end along the dimension named above; each array names one. Nothing has to cross between parts.
All inputs are finite; a program needn't handle non-finite values. No bound on the sum of `tile_mask` on one device may be relied on, other than what follows from the above.
Results may differ from a plain program's by a relative error of at most 0.0085.
Values may be sent and summed in bfloat16 or wider, within the bound.
A program may use at most 64 MiB of HBM per device.

v0:
```python
import math

import jax
import jax.numpy as jnp
from jax import lax
from jax.sharding import PartitionSpec as P

ITERS = 2


STEP_SIZE = 0.004


def from_behind(block, axis, distance):
    devices = range(lax.axis_size(axis))
    route = [((i - distance) % len(devices), i) for i in devices]
    return lax.ppermute(block, axis, route)


def per_device(rating_tiles, tile_mask, user_rows, item_rows, user_noise, item_noise):
    noise_scale = math.sqrt(STEP_SIZE)
    rounds = rating_tiles.shape[1]
    new_users = user_rows
    new_items = item_rows
    for sweep in range(ITERS):
        user_half = new_users.astype(jnp.bfloat16)
        item_block = lax.all_gather(new_items.astype(jnp.bfloat16), "ugrp", axis=0, tiled=True)
        user_grad = jnp.zeros(new_users.shape, jnp.float32)
        running = None
        for offset in range(rounds):
            if offset > 0:
                item_block = from_behind(item_block, "blk", 1)
            predicted = lax.dot_general(
                user_half, item_block, (((1,), (1,)), ((), ())), preferred_element_type=jnp.float32
            )
            rating = rating_tiles[:, offset, :].astype(jnp.float32)
            residual = jnp.where(
                tile_mask[:, offset, :] > 0, rating - predicted, jnp.float32(0.0)
            ).astype(jnp.bfloat16)
            user_grad = user_grad + jnp.dot(
                residual, item_block, preferred_element_type=jnp.float32
            )
            item_part = lax.dot_general(
                residual, user_half, (((0,), (0,)), ((), ())), preferred_element_type=jnp.float32
            )
            if offset == 0:
                running = item_part
            else:
                running = (
                    from_behind(running.astype(jnp.bfloat16), "blk", 1).astype(running.dtype)
                    + item_part
                )
        running = from_behind(running.astype(jnp.bfloat16), "blk", 1 - rounds).astype(running.dtype)
        item_grad = lax.psum_scatter(
            running.astype(jnp.bfloat16), "ugrp", scatter_dimension=0, tiled=True
        ).astype(jnp.float32)
        new_users = (
            new_users
            + 0.5 * STEP_SIZE * (user_grad - new_users)
            + noise_scale * user_noise[sweep].astype(jnp.float32)
        )
        new_items = (
            new_items
            + 0.5 * STEP_SIZE * (item_grad - new_items)
            + noise_scale * item_noise[sweep].astype(jnp.float32)
        )
    return (new_users, new_items)


def solution(mesh):
    return jax.shard_map(
        per_device,
        mesh=mesh,
        in_specs=(
            P(("parts", "blk", "ugrp"), None, None),
            P(("parts", "blk", "ugrp"), None, None),
            P(("parts", "blk", "ugrp"), None),
            P(("parts", "blk", "ugrp"), None),
            P(None, ("parts", "blk", "ugrp"), None),
            P(None, ("parts", "blk", "ugrp"), None),
        ),
        out_specs=(P(("parts", "blk", "ugrp"), None), P(("parts", "blk", "ugrp"), None)),
        check_vma=False,
    )
```

profile of v0, /device:TPU:0, one launch (start us, length us, event | category | flops | bytes accessed | tf_op | source)
XLA Modules:
  0.0 127.8 jit_solution(16484671415139405255)
XLA Ops:
  7.2 0.9 convert_element_type.135
  8.1 2.0 %all_gather.6 = bf16[256,256]{1,0:T(8,128)(2,1)S(1)} all-gather(bf16[128,256]{1,0:T(8,128)(2,1)S(1)} %convert_element_type.135), channel_id=1, replica_groups=mesh['parts'=2,'blk'=8,'ugrp'=2] {'ugrp'}, dimensions={0}, use_global_device_ids=true | all-gather | bytes 196608 | tf_op jit(solution)/shard_map/all_gather | solution.py:27
  10.1 2.8 %collective-permute-start = (bf16[256,256]{1,0:T(8,128)(2,1)S(1)}, bf16[256,256]{1,0:T(8,128)(2,1)S(1)}, u32[]{:S(2)}, u32[]{:S(2)}) collective-permute-start(bf16[256,256]{1,0:T(8,128)(2,1)S(1)} %all_gather.6), channel_id=1, source_target_pairs={{14,0},{0,2},{2,4},{4,6},{6,8},{8,10},{10,12},{12,14},{15,1},{1,3}... | collective-permute-start | bytes 393224 | tf_op jit(solution)/shard_map/ppermute | solution.py:17
  13.0 1.3 convert_element_type.134
  14.3 10.3 %fusion.29 = (s32[1024,1,256]{2,1,0:T(1,128)S(1)}, s32[1024,1,256]{2,1,0:T(1,128)S(1)}, s32[1024,1,256]{2,1,0:T(1,128)S(1)}, s32[1024,1,256]{2,1,0:T(1,128)S(1)}) fusion(s32[1024,4,256]{2,1,0:T(4,128)} %param.7), kind=kLoop, calls=%fused_computation.61 | loop fusion | bytes 8388608 | tf_op jit(solution)/shard_map/slice | solution.py:38
  24.5 3.1 %fusion.30 = (bf16[1024,1,256]{2,1,0:T(2,128)(2,1)S(1)}, bf16[1024,1,256]{2,1,0:T(2,128)(2,1)S(1)}, bf16[1024,1,256]{2,1,0:T(2,128)(2,1)S(1)}, bf16[1024,1,256]{2,1,0:T(2,128)(2,1)S(1)}) fusion(bf16[1024,4,256]{2,1,0:T(4,128)(2,1)S(1)} %copy-done), kind=kLoop, calls=%fused_computation.62 | loop fusion | bytes 4194304 | tf_op jit(solution)/shard_map/slice | solution.py:36
  27.6 0.3 fusion.16
  28.0 0.3 convolution_convert_fusion.1
  28.4 1.6 %collective-permute-start.3 = (bf16[256,256]{1,0:T(8,128)(2,1)S(1)}, bf16[256,256]{1,0:T(8,128)(2,1)S(1)}, u32[]{:S(2)}, u32[]{:S(2)}) collective-permute-start(bf16[256,256]{1,0:T(8,128)(2,1)S(1)} %convolution_convert_fusion.1), channel_id=1, source_target_pairs={{14,0},{0,2},{2,4},{4,6},{6,8},{8,10},{10,12},{12,14},{15,1},{1,3}... | collective-permute-start | bytes 393224 | tf_op jit(solution)/shard_map/ppermute | solution.py:17
  30.0 0.3 fusion.26
  30.6 0.4 fusion.17
  31.0 5.4 %collective-permute-done.3 = bf16[256,256]{1,0:T(8,128)(2,1)S(1)} collective-permute-done((bf16[256,256]{1,0:T(8,128)(2,1)S(1)}, bf16[256,256]{1,0:T(8,128)(2,1)S(1)}, u32[]{:S(2)}, u32[]{:S(2)}) %collective-permute-start.3) | collective-permute-done | bytes 131104 | tf_op jit(solution)/shard_map/ppermute | solution.py:17
  36.4 0.3 add_convert_fusion.5
  36.8 1.2 collective-permute-start.1
  38.3 8.4 %collective-permute-done.1 = bf16[256,256]{1,0:T(8,128)(2,1)S(1)} collective-permute-done((bf16[256,256]{1,0:T(8,128)(2,1)S(1)}, bf16[256,256]{1,0:T(8,128)(2,1)S(1)}, u32[]{:S(2)}, u32[]{:S(2)}) %collective-permute-start.1) | collective-permute-done | bytes 131104 | tf_op jit(solution)/shard_map/ppermute | solution.py:17
  46.7 0.4 fusion.18
  47.1 0.3 fusion.33
  47.6 6.8 %collective-permute-done.2 = bf16[256,256]{1,0:T(8,128)(2,1)S(1)} collective-permute-done((bf16[256,256]{1,0:T(8,128)(2,1)S(1)}, bf16[256,256]{1,0:T(8,128)(2,1)S(1)}, u32[]{:S(2)}, u32[]{:S(2)}) %collective-permute-start.2) | collective-permute-done | bytes 131104 | tf_op jit(solution)/shard_map/ppermute | solution.py:17
  54.4 0.4 fusion.19
  54.8 0.3 fusion.34
  55.2 1.4 %collective-permute-done.5 = bf16[256,256]{1,0:T(8,128)(2,1)S(1)} collective-permute-done((bf16[256,256]{1,0:T(8,128)(2,1)S(1)}, bf16[256,256]{1,0:T(8,128)(2,1)S(1)}, u32[]{:S(2)}, u32[]{:S(2)}) %collective-permute-start.5) | collective-permute-done | bytes 131104 | tf_op jit(solution)/shard_map/ppermute | solution.py:17
  56.7 1.3 convolution_add_fusion.4
  58.0 4.6 %collective-permute-done.6 = bf16[256,256]{1,0:T(8,128)(2,1)S(1)} collective-permute-done((bf16[256,256]{1,0:T(8,128)(2,1)S(1)}, bf16[256,256]{1,0:T(8,128)(2,1)S(1)}, u32[]{:S(2)}, u32[]{:S(2)}) %collective-permute-start.6) | collective-permute-done | bytes 131104 | tf_op jit(solution)/shard_map/ppermute | solution.py:17
  62.6 0.7 copy-done.18
  63.3 3.1 %fusion.31 = (bf16[1024,256]{1,0:T(8,128)(2,1)S(1)}, f32[1024,256]{1,0:T(8,128)}) fusion(bf16[2,1024,256]{2,1,0:T(8,128)(2,1)} %param.10, f32[1024,256]{1,0:T(8,128)} %param.8, f32[1024,256]{1,0:T(8,128)} %convolution_add_fusion.4, bf16[1024,256]{1,0:T(8,128)(2,1)S(1)} %fusion.19, bf16[256,256]{1,0:T(8,128)(2,1)S(1)} %collective-permute-done.2), kind=kOutput, calls=%fused_computation.63 | convolution fusion | flops 136314880 | bytes 4849664 | tf_op jit(solution)/shard_map/dot_general | solution.py:40
  66.4 4.2 %reduce-scatter.3.cloned.1.call-done = bf16[128,256]{1,0:T(8,128)(2,1)} async-done(((bf16[256,256]{1,0:T(8,128)(2,1)}), bf16[128,256]{1,0:T(8,128)(2,1)}) %reduce-scatter.3.cloned.1.call-update) | async-done | bytes 65552 | tf_op jit(solution)/shard_map/reduce_scatter | solution.py:54
  70.6 1.0 fusion.28
  71.6 1.9 %all_gather.7 = bf16[256,256]{1,0:T(8,128)(2,1)S(1)} all-gather(bf16[128,256]{1,0:T(8,128)(2,1)S(1)} %fusion.28), channel_id=1, replica_groups=mesh['parts'=2,'blk'=8,'ugrp'=2] {'ugrp'}, dimensions={0}, use_global_device_ids=true | all-gather | bytes 196608 | tf_op jit(solution)/shard_map/all_gather | solution.py:27
  73.5 1.7 %collective-permute-start.7 = (bf16[256,256]{1,0:T(8,128)(2,1)S(1)}, bf16[256,256]{1,0:T(8,128)(2,1)S(1)}, u32[]{:S(2)}, u32[]{:S(2)}) collective-permute-start(bf16[256,256]{1,0:T(8,128)(2,1)S(1)} %all_gather.7), channel_id=1, source_target_pairs={{14,0},{0,2},{2,4},{4,6},{6,8},{8,10},{10,12},{12,14},{15,1},{1,3}... | collective-permute-start | bytes 393224 | tf_op jit(solution)/shard_map/ppermute | solution.py:17
  75.2 1.6 %fusion.20 = bf16[1024,256]{1,0:T(8,128)(2,1)S(1)} fusion(bf16[1024,256]{1,0:T(8,128)(2,1)S(1)} %get-tuple-element.10, bf16[256,256]{1,0:T(8,128)(2,1)S(1)} %all_gather.7, bf16[1024,1,256]{2,1,0:T(2,128)(2,1)} %copy-done.4, s32[1024,1,256]{2,1,0:T(1,128)S(1)} %get-tuple-element.5), kind=kOutput, calls=%fused_computation.34 | convolution fusion | flops 135528448 | bytes 2752512 | tf_op jit(solution)/shard_map/dot_general | solution.py:33
  77.1 0.3 convolution_convert_fusion
  77.4 1.5 %collective-permute-start.10 = (bf16[256,256]{1,0:T(8,128)(2,1)S(1)}, bf16[256,256]{1,0:T(8,128)(2,1)S(1)}, u32[]{:S(2)}, u32[]{:S(2)}) collective-permute-start(bf16[256,256]{1,0:T(8,128)(2,1)S(1)} %convolution_convert_fusion), channel_id=1, source_target_pairs={{14,0},{0,2},{2,4},{4,6},{6,8},{8,10},{10,12},{12,14},{15,1},{1,3}... | collective-permute-start | bytes 393224 | tf_op jit(solution)/shard_map/ppermute | solution.py:17
  78.9 3.0 %collective-permute-done.7 = bf16[256,256]{1,0:T(8,128)(2,1)S(1)} collective-permute-done((bf16[256,256]{1,0:T(8,128)(2,1)S(1)}, bf16[256,256]{1,0:T(8,128)(2,1)S(1)}, u32[]{:S(2)}, u32[]{:S(2)}) %collective-permute-start.7) | collective-permute-done | bytes 131104 | tf_op jit(solution)/shard_map/ppermute | solution.py:17
  81.9 0.4 fusion.21
  82.3 3.3 %collective-permute-done.10 = bf16[256,256]{1,0:T(8,128)(2,1)S(1)} collective-permute-done((bf16[256,256]{1,0:T(8,128)(2,1)S(1)}, bf16[256,256]{1,0:T(8,128)(2,1)S(1)}, u32[]{:S(2)}, u32[]{:S(2)}) %collective-permute-start.10) | collective-permute-done | bytes 131104 | tf_op jit(solution)/shard_map/ppermute | solution.py:17
  85.6 0.3 add_convert_fusion.2
  86.0 1.1 collective-permute-start.8
  87.5 8.7 %collective-permute-done.8 = bf16[256,256]{1,0:T(8,128)(2,1)S(1)} collective-permute-done((bf16[256,256]{1,0:T(8,128)(2,1)S(1)}, bf16[256,256]{1,0:T(8,128)(2,1)S(1)}, u32[]{:S(2)}, u32[]{:S(2)}) %collective-permute-start.8) | collective-permute-done | bytes 131104 | tf_op jit(solution)/shard_map/ppermute | solution.py:17
  96.1 0.4 fusion.22
  96.6 0.3 fusion.36
  97.1 7.4 %collective-permute-done.9 = bf16[256,256]{1,0:T(8,128)(2,1)S(1)} collective-permute-done((bf16[256,256]{1,0:T(8,128)(2,1)S(1)}, bf16[256,256]{1,0:T(8,128)(2,1)S(1)}, u32[]{:S(2)}, u32[]{:S(2)}) %collective-permute-start.9) | collective-permute-done | bytes 131104 | tf_op jit(solution)/shard_map/ppermute | solution.py:17
  104.5 0.4 fusion.23
  104.9 0.3 fusion.37
  105.2 1.8 %collective-permute-done.12 = bf16[256,256]{1,0:T(8,128)(2,1)S(1)} collective-permute-done((bf16[256,256]{1,0:T(8,128)(2,1)S(1)}, bf16[256,256]{1,0:T(8,128)(2,1)S(1)}, u32[]{:S(2)}, u32[]{:S(2)}) %collective-permute-start.12) | collective-permute-done | bytes 131104 | tf_op jit(solution)/shard_map/ppermute | solution.py:17
  107.5 5.6 %collective-permute-done.13 = bf16[256,256]{1,0:T(8,128)(2,1)} collective-permute-done((bf16[256,256]{1,0:T(8,128)(2,1)S(1)}, bf16[256,256]{1,0:T(8,128)(2,1)}, u32[]{:S(2)}, u32[]{:S(2)}) %collective-permute-start.13) | collective-permute-done | bytes 131104 | tf_op jit(solution)/shard_map/ppermute | solution.py:17
  113.1 2.6 %fusion.3 = f32[1024,256]{1,0:T(8,128)} fusion(f32[1024,256]{1,0:T(8,128)S(1)} %copy-done.1, f32[1024,256]{1,0:T(8,128)S(1)} %convolution_add_fusion.1, bf16[1024,256]{1,0:T(8,128)(2,1)} %copy-done.5, bf16[256,256]{1,0:T(8,128)(2,1)} %copy-done.17, bf16[2,1024,256]{2,1,0:T(8,128)(2,1)} %param.10), kind=kOutput, calls=%fused_computation.4 | convolution fusion | flops 136052736 | bytes 4325376 | tf_op jit(solution)/shard_map/dot_general | solution.py:40
  115.8 3.6 %reduce-scatter.5.cloned.1.call-done = bf16[128,256]{1,0:T(8,128)(2,1)} async-done(((bf16[256,256]{1,0:T(8,128)(2,1)}), bf16[128,256]{1,0:T(8,128)(2,1)}) %reduce-scatter.5.cloned.1.call-update) | async-done | bytes 65552 | tf_op jit(solution)/shard_map/reduce_scatter | solution.py:54
  119.4 1.6 %bitcast_add_fusion = f32[128,256]{1,0:T(8,128)} fusion(bf16[128,256]{1,0:T(8,128)(2,1)} %reduce-scatter.5.cloned.1.call-done, bf16[2,128,256]{2,1,0:T(8,128)(2,1)S(1)} %copy-done.11, f32[128,256]{1,0:T(8,128)S(1)} %copy-done.6, bf16[128,256]{1,0:T(8,128)(2,1)S(1)} %copy-done.16), kind=kLoop, calls=%fused_computation.58 | loop fusion | flops 458752 | bytes 524288 | tf_op jit(solution)/shard_map/add | solution.py:63
  (61 shorter events, 2.2 us)
Async XLA Ops:
  7.2 63.4 %reduce-scatter.3.cloned.1.call-start = ((), (), s32[]{:S(2)}) async-start(), calls=%async_computation.2 | async-start | bytes 196608 | tf_op jit(solution)/shard_map/reduce_scatter | solution.py:54
  10.1 20.5 %collective-permute-start = (bf16[256,256]{1,0:T(8,128)(2,1)S(1)}, bf16[256,256]{1,0:T(8,128)(2,1)S(1)}, u32[]{:S(2)}, u32[]{:S(2)}) collective-permute-start(bf16[256,256]{1,0:T(8,128)(2,1)S(1)} %all_gather.6), channel_id=1, source_target_pairs={{14,0},{0,2},{2,4},{4,6},{6,8},{8,10},{10,12},{12,14},{15,1},{1,3}... | collective-permute-start | bytes 393224 | tf_op jit(solution)/shard_map/ppermute | solution.py:17
  14.2 10.3 %copy-start = (bf16[1024,4,256]{2,1,0:T(4,128)(2,1)S(1)}, bf16[1024,4,256]{2,1,0:T(4,128)(2,1)}, u32[]{:S(2)}) copy-start(bf16[1024,4,256]{2,1,0:T(4,128)(2,1)} %param.6) | copy-start | bytes 6291460
  27.6 2.4 %copy-start.4 = (bf16[1024,1,256]{2,1,0:T(2,128)(2,1)}, bf16[1024,1,256]{2,1,0:T(2,128)(2,1)S(1)}, u32[]{:S(2)}) copy-start(bf16[1024,1,256]{2,1,0:T(2,128)(2,1)S(1)} %get-tuple-element.9) | copy-start | bytes 1572868
  27.6 3.0 %copy-start.2 = (bf16[1024,1,256]{2,1,0:T(2,128)(2,1)}, bf16[1024,1,256]{2,1,0:T(2,128)(2,1)S(1)}, u32[]{:S(2)}) copy-start(bf16[1024,1,256]{2,1,0:T(2,128)(2,1)S(1)} %get-tuple-element.8) | copy-start | bytes 1572868
  27.6 19.1 %copy-start.9 = (bf16[1024,1,256]{2,1,0:T(2,128)(2,1)}, bf16[1024,1,256]{2,1,0:T(2,128)(2,1)S(1)}, u32[]{:S(2)}) copy-start(bf16[1024,1,256]{2,1,0:T(2,128)(2,1)S(1)} %get-tuple-element.7) | copy-start | bytes 1572868
  27.6 26.8 %copy-start.7 = (bf16[1024,1,256]{2,1,0:T(2,128)(2,1)}, bf16[1024,1,256]{2,1,0:T(2,128)(2,1)S(1)}, u32[]{:S(2)}) copy-start(bf16[1024,1,256]{2,1,0:T(2,128)(2,1)S(1)} %get-tuple-element.6) | copy-start | bytes 1572868
  28.4 8.0 %collective-permute-start.3 = (bf16[256,256]{1,0:T(8,128)(2,1)S(1)}, bf16[256,256]{1,0:T(8,128)(2,1)S(1)}, u32[]{:S(2)}, u32[]{:S(2)}) collective-permute-start(bf16[256,256]{1,0:T(8,128)(2,1)S(1)} %convolution_convert_fusion.1), channel_id=1, source_target_pairs={{14,0},{0,2},{2,4},{4,6},{6,8},{8,10},{10,12},{12,14},{15,1},{1,3}... | collective-permute-start | bytes 393224 | tf_op jit(solution)/shard_map/ppermute | solution.py:17
  30.3 16.5 %copy-start.14 = (pred[1024,256]{1,0:T(32,128)(4,1)}, pred[1024,256]{1,0:T(32,128)(4,1)S(1)}, u32[]{:S(2)}) copy-start(pred[1024,256]{1,0:T(32,128)(4,1)S(1)} %get-tuple-element.12) | copy-start | bytes 786436
  30.3 24.1 %copy-start.12 = (pred[1024,256]{1,0:T(32,128)(4,1)}, pred[1024,256]{1,0:T(32,128)(4,1)S(1)}, u32[]{:S(2)}) copy-start(pred[1024,256]{1,0:T(32,128)(4,1)S(1)} %get-tuple-element.13) | copy-start | bytes 786436
  36.7 10.7 %collective-permute-start.4 = (bf16[256,256]{1,0:T(8,128)(2,1)S(1)}, bf16[256,256]{1,0:T(8,128)(2,1)S(1)}, u32[]{:S(2)}, u32[]{:S(2)}) collective-permute-start(bf16[256,256]{1,0:T(8,128)(2,1)S(1)} %add_convert_fusion.5), channel_id=1, source_target_pairs={{14,0},{0,2},{2,4},{4,6},{6,8},{8,10},{10,12},{12,14},{15,1},{1,3}... | collective-permute-start | bytes 393224 | tf_op jit(solution)/shard_map/ppermute | solution.py:17
  36.8 9.9 %collective-permute-start.1 = (bf16[256,256]{1,0:T(8,128)(2,1)S(1)}, bf16[256,256]{1,0:T(8,128)(2,1)S(1)}, u32[]{:S(2)}, u32[]{:S(2)}) collective-permute-start(bf16[256,256]{1,0:T(8,128)(2,1)S(1)} %collective-permute-done), channel_id=1, source_target_pairs={{14,0},{0,2},{2,4},{4,6},{6,8},{8,10},{10,12},{12,14},{15,1},{1,3}... | collective-permute-start | bytes 393224 | tf_op jit(solution)/shard_map/ppermute | solution.py:17
  46.7 7.7 %collective-permute-start.2 = (bf16[256,256]{1,0:T(8,128)(2,1)S(1)}, bf16[256,256]{1,0:T(8,128)(2,1)S(1)}, u32[]{:S(2)}, u32[]{:S(2)}) collective-permute-start(bf16[256,256]{1,0:T(8,128)(2,1)S(1)} %collective-permute-done.1), channel_id=1, source_target_pairs={{14,0},{0,2},{2,4},{4,6},{6,8},{8,10},{10,12},{12,14},{15,1},{1,3}... | collective-permute-start | bytes 393224 | tf_op jit(solution)/shard_map/ppermute | solution.py:17
  47.5 9.1 %collective-permute-start.5 = (bf16[256,256]{1,0:T(8,128)(2,1)S(1)}, bf16[256,256]{1,0:T(8,128)(2,1)S(1)}, u32[]{:S(2)}, u32[]{:S(2)}) collective-permute-start(bf16[256,256]{1,0:T(8,128)(2,1)S(1)} %add_convert_fusion.4), channel_id=1, source_target_pairs={{14,0},{0,2},{2,4},{4,6},{6,8},{8,10},{10,12},{12,14},{15,1},{1,3}... | collective-permute-start | bytes 393224 | tf_op jit(solution)/shard_map/ppermute | solution.py:17
  55.2 15.4 %copy-start.6 = (f32[128,256]{1,0:T(8,128)S(1)}, f32[128,256]{1,0:T(8,128)}, u32[]{:S(2)}) copy-start(f32[128,256]{1,0:T(8,128)} %param.9) | copy-start | bytes 393220
  55.2 15.4 %copy-start.11 = (bf16[2,128,256]{2,1,0:T(8,128)(2,1)S(1)}, bf16[2,128,256]{2,1,0:T(8,128)(2,1)}, u32[]{:S(2)}) copy-start(bf16[2,128,256]{2,1,0:T(8,128)(2,1)} %param.11) | copy-start | bytes 393220
  56.7 5.9 %collective-permute-start.6 = (bf16[256,256]{1,0:T(8,128)(2,1)S(1)}, bf16[256,256]{1,0:T(8,128)(2,1)S(1)}, u32[]{:S(2)}, u32[]{:S(2)}) collective-permute-start(bf16[256,256]{1,0:T(8,128)(2,1)S(1)} %add_convert_fusion.3), channel_id=1, source_target_pairs={{6,0},{8,2},{10,4},{12,6},{14,8},{0,10},{2,12},{4,14},{7,1},{9,3},... | collective-permute-start | bytes 393224 | tf_op jit(solution)/shard_map/ppermute | solution.py:17
  62.6 0.7 copy-start.18
  63.3 56.2 %reduce-scatter.5.cloned.1.call-start = ((), (), s32[]{:S(2)}) async-start(), calls=%async_computation.3 | async-start | bytes 196608 | tf_op jit(solution)/shard_map/reduce_scatter | solution.py:54
  70.6 11.3 %copy-start.3 = (bf16[1024,1,256]{2,1,0:T(2,128)(2,1)S(1)}, bf16[1024,1,256]{2,1,0:T(2,128)(2,1)}, u32[]{:S(2)}) copy-start(bf16[1024,1,256]{2,1,0:T(2,128)(2,1)} %copy-done.2) | copy-start | bytes 1572868
  73.5 8.4 %collective-permute-start.7 = (bf16[256,256]{1,0:T(8,128)(2,1)S(1)}, bf16[256,256]{1,0:T(8,128)(2,1)S(1)}, u32[]{:S(2)}, u32[]{:S(2)}) collective-permute-start(bf16[256,256]{1,0:T(8,128)(2,1)S(1)} %all_gather.7), channel_id=1, source_target_pairs={{14,0},{0,2},{2,4},{4,6},{6,8},{8,10},{10,12},{12,14},{15,1},{1,3}... | collective-permute-start | bytes 393224 | tf_op jit(solution)/shard_map/ppermute | solution.py:17
  77.0 19.1 %copy-start.10 = (bf16[1024,1,256]{2,1,0:T(2,128)(2,1)S(1)}, bf16[1024,1,256]{2,1,0:T(2,128)(2,1)}, u32[]{:S(2)}) copy-start(bf16[1024,1,256]{2,1,0:T(2,128)(2,1)} %copy-done.9) | copy-start | bytes 1572868
  77.1 19.1 %copy-start.15 = (pred[1024,256]{1,0:T(32,128)(4,1)S(1)}, pred[1024,256]{1,0:T(32,128)(4,1)}, u32[]{:S(2)}) copy-start(pred[1024,256]{1,0:T(32,128)(4,1)} %copy-done.14) | copy-start | bytes 786436
  77.4 8.2 %collective-permute-start.10 = (bf16[256,256]{1,0:T(8,128)(2,1)S(1)}, bf16[256,256]{1,0:T(8,128)(2,1)S(1)}, u32[]{:S(2)}, u32[]{:S(2)}) collective-permute-start(bf16[256,256]{1,0:T(8,128)(2,1)S(1)} %convolution_convert_fusion), channel_id=1, source_target_pairs={{14,0},{0,2},{2,4},{4,6},{6,8},{8,10},{10,12},{12,14},{15,1},{1,3}... | collective-permute-start | bytes 393224 | tf_op jit(solution)/shard_map/ppermute | solution.py:17
  82.3 22.2 %copy-start.8 = (bf16[1024,1,256]{2,1,0:T(2,128)(2,1)S(1)}, bf16[1024,1,256]{2,1,0:T(2,128)(2,1)}, u32[]{:S(2)}) copy-start(bf16[1024,1,256]{2,1,0:T(2,128)(2,1)} %copy-done.7) | copy-start | bytes 1572868
  82.3 22.2 %copy-start.13 = (pred[1024,256]{1,0:T(32,128)(4,1)S(1)}, pred[1024,256]{1,0:T(32,128)(4,1)}, u32[]{:S(2)}) copy-start(pred[1024,256]{1,0:T(32,128)(4,1)} %copy-done.12) | copy-start | bytes 786436
  86.0 11.0 %collective-permute-start.11 = (bf16[256,256]{1,0:T(8,128)(2,1)S(1)}, bf16[256,256]{1,0:T(8,128)(2,1)S(1)}, u32[]{:S(2)}, u32[]{:S(2)}) collective-permute-start(bf16[256,256]{1,0:T(8,128)(2,1)S(1)} %add_convert_fusion.2), channel_id=1, source_target_pairs={{14,0},{0,2},{2,4},{4,6},{6,8},{8,10},{10,12},{12,14},{15,1},{1,3}... | collective-permute-start | bytes 393224 | tf_op jit(solution)/shard_map/ppermute | solution.py:17
  86.0 10.1 %collective-permute-start.8 = (bf16[256,256]{1,0:T(8,128)(2,1)S(1)}, bf16[256,256]{1,0:T(8,128)(2,1)S(1)}, u32[]{:S(2)}, u32[]{:S(2)}) collective-permute-start(bf16[256,256]{1,0:T(8,128)(2,1)S(1)} %collective-permute-done.7), channel_id=1, source_target_pairs={{14,0},{0,2},{2,4},{4,6},{6,8},{8,10},{10,12},{12,14},{15,1},{1,3}... | collective-permute-start | bytes 393224 | tf_op jit(solution)/shard_map/ppermute | solution.py:17
  96.5 16.6 %copy-start.1 = (f32[1024,256]{1,0:T(8,128)S(1)}, f32[1024,256]{1,0:T(8,128)}, u32[]{:S(2)}) copy-start(f32[1024,256]{1,0:T(8,128)} %get-tuple-element.11) | copy-start | bytes 3145732
  96.5 7.9 %collective-permute-start.9 = (bf16[256,256]{1,0:T(8,128)(2,1)S(1)}, bf16[256,256]{1,0:T(8,128)(2,1)S(1)}, u32[]{:S(2)}, u32[]{:S(2)}) collective-permute-start(bf16[256,256]{1,0:T(8,128)(2,1)S(1)} %collective-permute-done.8), channel_id=1, source_target_pairs={{14,0},{0,2},{2,4},{4,6},{6,8},{8,10},{10,12},{12,14},{15,1},{1,3}... | collective-permute-start | bytes 393224 | tf_op jit(solution)/shard_map/ppermute | solution.py:17
  97.0 10.1 %collective-permute-start.12 = (bf16[256,256]{1,0:T(8,128)(2,1)S(1)}, bf16[256,256]{1,0:T(8,128)(2,1)S(1)}, u32[]{:S(2)}, u32[]{:S(2)}) collective-permute-start(bf16[256,256]{1,0:T(8,128)(2,1)S(1)} %add_convert_fusion.1), channel_id=1, source_target_pairs={{14,0},{0,2},{2,4},{4,6},{6,8},{8,10},{10,12},{12,14},{15,1},{1,3}... | collective-permute-start | bytes 393224 | tf_op jit(solution)/shard_map/ppermute | solution.py:17
  104.5 3.0 %copy-start.17 = (bf16[256,256]{1,0:T(8,128)(2,1)}, bf16[256,256]{1,0:T(8,128)(2,1)S(1)}, u32[]{:S(2)}) copy-start(bf16[256,256]{1,0:T(8,128)(2,1)S(1)} %collective-permute-done.9) | copy-start | bytes 393220
  104.9 2.6 %copy-start.5 = (bf16[1024,256]{1,0:T(8,128)(2,1)}, bf16[1024,256]{1,0:T(8,128)(2,1)S(1)}, u32[]{:S(2)}) copy-start(bf16[1024,256]{1,0:T(8,128)(2,1)S(1)} %fusion.23) | copy-start | bytes 1572868
  105.2 14.2 %copy-start.16 = (bf16[128,256]{1,0:T(8,128)(2,1)S(1)}, bf16[128,256]{1,0:T(8,128)(2,1)}, u32[]{:S(2)}) copy-start(bf16[128,256]{1,0:T(8,128)(2,1)} %reduce-scatter.3.cloned.1.call-done) | copy-start | bytes 196612
  107.1 6.0 %collective-permute-start.13 = (bf16[256,256]{1,0:T(8,128)(2,1)S(1)}, bf16[256,256]{1,0:T(8,128)(2,1)}, u32[]{:S(2)}, u32[]{:S(2)}) collective-permute-start(bf16[256,256]{1,0:T(8,128)(2,1)S(1)} %add_convert_fusion), channel_id=1, source_target_pairs={{6,0},{8,2},{10,4},{12,6},{14,8},{0,10},{2,12},{4,14},{7,1},{9,3},... | collective-permute-start | bytes 393224 | tf_op jit(solution)/shard_map/ppermute | solution.py:17
Sparse Core Ops, SparseCore 0:
  63.4 7.1 reduce-scatter.2
  113.2 6.1 reduce-scatter.4
where the time goes:
time: 128 us
  waiting for transfers between devices  64.3 us (50%)
  matrix products  15.4 us (12%)
  between operations  14.5 us (11%)
  local copies, waits for them, and re-layouts  14.1 us (11%)
  starting transfers between devices  10.5 us (8%)
  other arithmetic  5.14 us (4%)
  blocking collectives  3.9 us (3%)
    ppermute x14, waiting for transfers between devices, from_behind(): return lax.ppermute(block, axis, route)  56.4 us
    ppermute x14, starting transfers between devices, from_behind(): return lax.ppermute(block, axis, route)  10.4 us
    slice x1, local copies, waits for them, and re-layouts, per_device(): tile_mask[:, offset, :] > 0  10.3 us
    dot_general x8, matrix products, per_device(): jnp.dot(residual, item_block, preferred_element_type=jnp.float32)  8.45 us
    reduce_scatter x2, waiting for transfers between devices, per_device(): lax.psum_scatter(running.astype(jnp.bfloat16), 'ugrp', scatter_dimension=...  7.85 us
    dot_general x8, matrix products, per_device(): lax.dot_general(user_half, item_block, (((1,), (1,)), ((), ())), preferre...  4.24 us
    all_gather x2, blocking collectives, per_device(): lax.all_gather(new_items.astype(jnp.bfloat16), 'ugrp', axis=0, tiled=True)  3.9 us
    slice x1, local copies, waits for them, and re-layouts, per_device(): rating = rating_tiles[:, offset, :].astype(jnp.float32)  3.05 us
  transfers between devices with their start and end apart: 16, of which 13 were waited for; matrix products, arithmetic and copies ran while one was open for 23% of the time, Pallas kernels for 0%

commit v1 on v0

v1 whole, which is shorter than its diff:
```python
import functools
import math

import jax
import jax.numpy as jnp
from jax import lax
from jax.experimental import pallas as pl
from jax.experimental.pallas import tpu as pltpu
from jax.sharding import PartitionSpec as P

ITERS = 2

STEP_SIZE = 0.004

UNSEEN = 64.0


def nt(a, b):
    return lax.dot_general(a, b, (((1,), (1,)), ((), ())), preferred_element_type=jnp.float32)


def nn(a, b):
    return jnp.dot(a, b, preferred_element_type=jnp.float32)


def kernel(
    positions,
    rating_hbm, mask_hbm, users_hbm, items_hbm, unoise_hbm, inoise_hbm,
    out_users_hbm, out_items_hbm,
    rating_v, mask_v, users_v, items_v, unoise_v, inoise_v,
    seen_v, uhalf_v, ut_v, resid_v, block_v,
    own_v, xsend_v, xrecv_v, gsend_v, grecv_v,
    local_sem, bsend_sem, brecv_sem, fsend_sem, frecv_sem,
    xsend_sem, xrecv_sem, gsend_sem, grecv_sem,
):
    noise_scale = math.sqrt(STEP_SIZE)
    n_users, rounds, ib = rating_v.shape
    half = ib // 2
    h = lax.axis_index("blk")
    c = lax.axis_index("ugrp")
    o = 1 - c
    mine = pl.ds(pl.multiple_of(c * half, half), half)

    def ahead(d):
        return {"blk": lax.rem(h + d, positions)}

    def behind(d):
        return {"blk": lax.rem(h + positions - d, positions)}

    other = {"ugrp": o}

    loads = []
    for i, (src, dst) in enumerate((
        (items_hbm, items_v), (users_hbm, users_v), (rating_hbm, rating_v),
        (mask_hbm, mask_v), (inoise_hbm, inoise_v), (unoise_hbm, unoise_v),
    )):
        load = pltpu.make_async_copy(src, dst, local_sem.at[i])
        load.start()
        loads.append(load)

    barrier = pltpu.get_barrier_semaphore()
    peers = [other] + [ahead(d) for d in range(1, rounds)] + [behind(d) for d in range(1, rounds)]
    for peer in peers:
        pl.semaphore_signal(barrier, inc=1, device_id=peer, device_id_type=pl.DeviceIdType.MESH)
    pl.semaphore_wait(barrier, len(peers))

    def remote(src, dst, send, recv, to):
        return pltpu.make_async_remote_copy(
            src_ref=src, dst_ref=dst, send_sem=send, recv_sem=recv,
            device_id=to, device_id_type=pl.DeviceIdType.MESH,
        )

    sent = []
    loads[0].wait()
    for t in range(ITERS):
        block_v[t, 0, mine, :] = items_v[...].astype(jnp.bfloat16)
        held = block_v.at[t, 0, mine, :]
        hops = []
        for d in range(1, rounds):
            hop = remote(held, block_v.at[t, d, mine, :], bsend_sem.at[t, d], brecv_sem.at[t, d], ahead(d))
            hop.start()
            hops.append(hop)
            sent.append(hop)
        forwards = []
        for d in range(rounds):
            forwards.append(remote(
                block_v.at[t, d, mine, :], block_v.at[t, d, mine, :],
                fsend_sem.at[t, d], frecv_sem.at[t, d], other,
            ))
            sent.append(forwards[d])
        forwards[0].start()

        if t == 0:
            loads[1].wait()
        uhalf_v[...] = users_v[...].astype(jnp.bfloat16)
        ut_v[...] = uhalf_v[...].T
        if t == 0:
            loads[2].wait()
            loads[3].wait()

            @pl.loop(0, n_users // 32)
            def _(i):
                rows = pl.ds(pl.multiple_of(i * 32, 32), 32)
                seen = jnp.where(mask_v[rows] > 0, rating_v[rows].astype(jnp.float32), UNSEEN)
                seen_v[:, rows, :] = jnp.swapaxes(seen, 0, 1).astype(jnp.bfloat16)

        exchanges = []
        for d in range(rounds):
            if d + 1 < rounds:
                hops[d].wait_recv()
                forwards[d + 1].start()
            forwards[d].wait_recv()
            block = block_v[t, d]
            for r in range(0, n_users, 256):
                rows = pl.ds(r, 256)
                predicted = nt(uhalf_v[rows, :], block)
                seen = seen_v[d, rows, :].astype(jnp.float32)
                resid_v[d, rows, :] = jnp.where(seen < UNSEEN, seen - predicted, 0.0).astype(jnp.bfloat16)
            part = nn(ut_v[...], resid_v[d])
            low, high = part[:, :half], part[:, half:]
            own_v[d] = jnp.where(c == 0, low, high)
            xsend_v[t, d] = jnp.where(c == 0, high, low).astype(jnp.bfloat16)
            exchange = remote(xsend_v.at[t, d], xrecv_v.at[t, d], xsend_sem.at[t, d], xrecv_sem.at[t, d], other)
            exchange.start()
            exchanges.append(exchange)
            sent.append(exchange)
        terms = []
        for d in range(1, rounds):
            exchanges[d].wait_recv()
            gsend_v[t, d] = (own_v[d] + xrecv_v[t, d].astype(jnp.float32)).astype(jnp.bfloat16)
            term = remote(gsend_v.at[t, d], grecv_v.at[t, d], gsend_sem.at[t, d], grecv_sem.at[t, d], behind(d))
            term.start()
            terms.append(term)
            sent.append(term)

        if t == 0:
            loads[5].wait()
        for r in range(0, n_users, 256):
            rows = pl.ds(r, 256)
            grad = nn(resid_v[0, rows, :], block_v[t, 0])
            for d in range(1, rounds):
                grad = grad + nn(resid_v[d, rows, :], block_v[t, d])
            users = users_v[rows, :]
            users_v[rows, :] = (
                users + 0.5 * STEP_SIZE * (grad - users)
                + noise_scale * unoise_v[t, rows, :].astype(jnp.float32)
            )
        if t == ITERS - 1:
            put_users = pltpu.make_async_copy(users_v, out_users_hbm, local_sem.at[0])
            put_users.start()

        if t == 0:
            loads[4].wait()
        exchanges[0].wait_recv()
        total = own_v[0] + xrecv_v[t, 0].astype(jnp.float32)
        for d in range(1, rounds):
            terms[d - 1].wait_recv()
            total = total + grecv_v[t, d].astype(jnp.float32)
        items = items_v[...]
        items_v[...] = (
            items + 0.5 * STEP_SIZE * (total.T - items)
            + noise_scale * inoise_v[t].astype(jnp.float32)
        )
    put_items = pltpu.make_async_copy(items_v, out_items_hbm, local_sem.at[1])
    put_items.start()
    for copy in sent:
        copy.wait_send()
    put_users.wait()
    put_items.wait()


def per_device(rating_tiles, tile_mask, user_rows, item_rows, user_noise, item_noise):
    n_users, rounds, ib = rating_tiles.shape
    n_items, rank = item_rows.shape
    half = ib // 2
    bf16, f32 = jnp.bfloat16, jnp.float32
    dma = pltpu.SemaphoreType.DMA
    return pl.pallas_call(
        functools.partial(kernel, lax.axis_size("blk")),
        out_shape=(
            jax.ShapeDtypeStruct(user_rows.shape, f32),
            jax.ShapeDtypeStruct(item_rows.shape, f32),
        ),
        in_specs=[pl.BlockSpec(memory_space=pl.ANY)] * 6,
        out_specs=[pl.BlockSpec(memory_space=pl.ANY)] * 2,
        scratch_shapes=[
            pltpu.VMEM(rating_tiles.shape, bf16),
            pltpu.VMEM(tile_mask.shape, jnp.int32),
            pltpu.VMEM(user_rows.shape, f32),
            pltpu.VMEM(item_rows.shape, f32),
            pltpu.VMEM(user_noise.shape, bf16),
            pltpu.VMEM(item_noise.shape, bf16),
            pltpu.VMEM((rounds, n_users, ib), bf16),
            pltpu.VMEM((n_users, rank), bf16),
            pltpu.VMEM((rank, n_users), bf16),
            pltpu.VMEM((rounds, n_users, ib), bf16),
            pltpu.VMEM((ITERS, rounds, ib, rank), bf16),
            pltpu.VMEM((rounds, rank, half), f32),
            pltpu.VMEM((ITERS, rounds, rank, half), bf16),
            pltpu.VMEM((ITERS, rounds, rank, half), bf16),
            pltpu.VMEM((ITERS, rounds, rank, half), bf16),
            pltpu.VMEM((ITERS, rounds, rank, half), bf16),
            dma((6,)),
        ] + [dma((ITERS, rounds))] * 8,
        compiler_params=pltpu.CompilerParams(
            collective_id=0, has_side_effects=True, vmem_limit_bytes=60 << 20,
        ),
        cost_estimate=pl.CostEstimate(
            flops=ITERS * rounds * 6 * n_users * ib * rank, bytes_accessed=10 << 20, transcendentals=0,
        ),
    )(rating_tiles, tile_mask, user_rows, item_rows, user_noise, item_noise)


def solution(mesh):
    spec = P(("parts", "blk", "ugrp"), None)
    tiles = P(("parts", "blk", "ugrp"), None, None)
    noise = P(None, ("parts", "blk", "ugrp"), None)
    return jax.shard_map(
        per_device,
        mesh=mesh,
        in_specs=(tiles, tiles, spec, spec, noise, noise),
        out_specs=(spec, spec),
        check_vma=False,
    )
```

time: 128 us -> 44.1 us (0.34)
  waiting for transfers between devices: 64.3 us -> 0 us
  Pallas kernels: 0 us -> 39.5 us
  matrix products: 15.4 us -> 0 us
  between operations: 14.5 us -> 0.64 us
  starting transfers between devices: 10.5 us -> 0 us
  local copies, waits for them, and re-layouts: 14.1 us -> 3.83 us
  other arithmetic: 5.14 us -> 0 us
  blocking collectives: 3.9 us -> 0 us
    ppermute x14 -> x0, waiting for transfers between devices: 56.4 us -> none  [from_behind(): return lax.ppermute(block, axis, route)]
    pallas_call x0 -> x1, Pallas kernels: none -> 39.5 us  [per_device(): pl.pallas_call(functools.partial(kernel, lax.axis_size('blk')), out_shape...]
    dot_general x24 -> x0, matrix products: 15.4 us -> none  [the longest x8 8.45 us: per_device(): jnp.dot(residual, item_block, preferred_element_type=jnp.float32)]
    slice x2 -> x0, local copies, waits for them, and re-layouts: 13.3 us -> none  [the longest x1 10.3 us: per_device(): tile_mask[:, offset, :] > 0]
    ppermute x14 -> x0, starting transfers between devices: 10.4 us -> none  [from_behind(): return lax.ppermute(block, axis, route)]
    reduce_scatter x2 -> x0, waiting for transfers between devices: 7.85 us -> none  [per_device(): lax.psum_scatter(running.astype(jnp.bfloat16), 'ugrp', scatter_dimension=...]
    all_gather x2 -> x0, blocking collectives: 3.9 us -> none  [per_device(): lax.all_gather(new_items.astype(jnp.bfloat16), 'ugrp', axis=0, tiled=True)]
    convert_element_type x7 -> x0, other arithmetic: 3.28 us -> none  [the longest x2 1.88 us: per_device(): new_items.astype(jnp.bfloat16)]
  transfers between devices with their start and end apart: 16 -> 0, of which waited for: 13 -> 0; matrix products, arithmetic and copies ran while one was open for 23% -> 0% of each run, Pallas kernels for 0% -> 0%
where the time goes in v1:
time: 44.1 us; the launch traced here: 43.9 us
  Pallas kernels  39.5 us (90%)
  local copies, waits for them, and re-layouts  3.83 us (9%)
  between operations  0.64 us (1%)
    pallas_call x1, Pallas kernels, per_device(): pl.pallas_call(functools.partial(kernel, lax.axis_size('blk')), out_shape...  39.5 us
    unnamed x2, local copies, waits for them, and re-layouts  3.83 us

profile of v1, /device:TPU:0, one launch (start us, length us, event | category | flops | bytes accessed | tf_op | source)
XLA Modules:
  0.0 43.9 jit_solution(17445214983055307788)
XLA Ops:
  0.6 39.5 %shard_map.77 = (f32[1024,256]{1,0:T(8,128)}, f32[128,256]{1,0:T(8,128)}) custom-call(bf16[1024,4,256]{2,1,0:T(4,128)(2,1)} %rating_hbm.1, s32[1024,4,256]{2,1,0:T(4,128)} %mask_hbm.1, f32[1024,256]{1,0:T(8,128)} %users_hbm.1, f32[128,256]{1,0:T(8,128)} %items_hbm.1, bf16[2,1024,256]{2,1,0:T(8,128)(2,1)} %unoise_hbm.1, bf16[2,128,256]{2,1,0:T(8,128)(2,1)} %inoise_hbm.1), custom_call_target="tpu_custom_call" | custom-call | flops 3221225472 | bytes 10485760 | tf_op jit(solution)/shard_map/pallas_call | solution.py:178
  40.1 2.3 %copy.10 = f32[1024,256]{1,0:T(8,128)} copy(f32[1024,256]{1,0:T(8,128)} %get-tuple-element.4) | data formatting | bytes 2097152
  42.4 1.6 %copy.11 = f32[128,256]{1,0:T(8,128)} copy(f32[128,256]{1,0:T(8,128)} %get-tuple-element.5) | data formatting | bytes 262144

commit v2 on v1

--- a/solution.py
+++ b/solution.py
@@ -12,6 +12,8 @@
 
 STEP_SIZE = 0.004
 
+PIECES = 1
+
 UNSEEN = 64.0
 
 
@@ -26,8 +28,8 @@
 def kernel(
     positions,
     rating_hbm, mask_hbm, users_hbm, items_hbm, unoise_hbm, inoise_hbm,
-    out_users_hbm, out_items_hbm,
-    rating_v, mask_v, users_v, items_v, unoise_v, inoise_v,
+    users_v, items_v,
+    rating_v, mask_v, unoise_v, inoise_v,
     seen_v, uhalf_v, ut_v, resid_v, block_v,
     own_v, xsend_v, xrecv_v, gsend_v, grecv_v,
     local_sem, bsend_sem, brecv_sem, fsend_sem, frecv_sem,
@@ -71,16 +73,26 @@
         )
 
     sent = []
+    rank = items_v.shape[1]
+
+    def spread(t, pieces, p):
+        width = rank // pieces
+        part = pl.ds(p * width, width)
+        block_v[t, 0, mine, part] = items_v[:, part].astype(jnp.bfloat16)
+        held = block_v.at[t, 0, mine, part]
+        started = []
+        for d in range(1, rounds):
+            hop = remote(
+                held, block_v.at[t, d, mine, part], bsend_sem.at[t, d, p], brecv_sem.at[t, d, p], ahead(d)
+            )
+            hop.start()
+            started.append(hop)
+            sent.append(hop)
+        return started
+
     loads[0].wait()
+    hops = [spread(0, 1, 0)]
     for t in range(ITERS):
-        block_v[t, 0, mine, :] = items_v[...].astype(jnp.bfloat16)
-        held = block_v.at[t, 0, mine, :]
-        hops = []
-        for d in range(1, rounds):
-            hop = remote(held, block_v.at[t, d, mine, :], bsend_sem.at[t, d], brecv_sem.at[t, d], ahead(d))
-            hop.start()
-            hops.append(hop)
-            sent.append(hop)
         forwards = []
         for d in range(rounds):
             forwards.append(remote(
@@ -104,11 +116,14 @@
                 seen = jnp.where(mask_v[rows] > 0, rating_v[rows].astype(jnp.float32), UNSEEN)
                 seen_v[:, rows, :] = jnp.swapaxes(seen, 0, 1).astype(jnp.bfloat16)
 
-        exchanges = []
-        for d in range(rounds):
-            if d + 1 < rounds:
-                hops[d].wait_recv()
-                forwards[d + 1].start()
+        exchanges, terms = [], []
+
+        def arrive(d):
+            for piece in hops:
+                piece[d - 1].wait_recv()
+            forwards[d].start()
+
+        def work(d):
             forwards[d].wait_recv()
             block = block_v[t, d]
             for r in range(0, n_users, 256):
@@ -124,14 +139,29 @@
             exchange.start()
             exchanges.append(exchange)
             sent.append(exchange)
-        terms = []
-        for d in range(1, rounds):
+
+        def send(d):
             exchanges[d].wait_recv()
             gsend_v[t, d] = (own_v[d] + xrecv_v[t, d].astype(jnp.float32)).astype(jnp.bfloat16)
-            term = remote(gsend_v.at[t, d], grecv_v.at[t, d], gsend_sem.at[t, d], grecv_sem.at[t, d], behind(d))
-            term.start()
-            terms.append(term)
-            sent.append(term)
+            started = []
+            for p in range(PIECES):
+                part = pl.ds(p * (rank // PIECES), rank // PIECES)
+                term = remote(
+                    gsend_v.at[t, d, part, :], grecv_v.at[t, d, part, :],
+                    gsend_sem.at[t, d, p], grecv_sem.at[t, d, p], behind(d),
+                )
+                term.start()
+                started.append(term)
+                sent.append(term)
+            terms.append(started)
+
+        work(0)
+        for d in range(1, rounds):
+            arrive(d)
+            if d > 1:
+                send(d - 1)
+            work(d)
+        send(rounds - 1)
 
         if t == 0:
             loads[5].wait()
@@ -145,28 +175,36 @@
                 users + 0.5 * STEP_SIZE * (grad - users)
                 + noise_scale * unoise_v[t, rows, :].astype(jnp.float32)
             )
-        if t == ITERS - 1:
-            put_users = pltpu.make_async_copy(users_v, out_users_hbm, local_sem.at[0])
-            put_users.start()
-
         if t == 0:
             loads[4].wait()
         exchanges[0].wait_recv()
-        total = own_v[0] + xrecv_v[t, 0].astype(jnp.float32)
-        for d in range(1, rounds):
-            terms[d - 1].wait_recv()
-            total = total + grecv_v[t, d].astype(jnp.float32)
-        items = items_v[...]
-        items_v[...] = (
-            items + 0.5 * STEP_SIZE * (total.T - items)
-            + noise_scale * inoise_v[t].astype(jnp.float32)
-        )
-    put_items = pltpu.make_async_copy(items_v, out_items_hbm, local_sem.at[1])
-    put_items.start()
+        hops = []
+        for p in range(PIECES):
+            part = pl.ds(p * (rank // PIECES), rank // PIECES)
+            total = own_v[0, part, :] + xrecv_v[t, 0, part, :].astype(jnp.float32)
+            for d in range(1, rounds):
+                terms[d - 1][p].wait_recv()
+                total = total + grecv_v[t, d, part, :].astype(jnp.float32)
+            items = items_v[:, part]
+            items_v[:, part] = (
+                items + 0.5 * STEP_SIZE * (total.T - items)
+                + noise_scale * inoise_v[t, :, part].astype(jnp.float32)
+            )
+            if t + 1 < ITERS:
+                hops.append(spread(t + 1, PIECES, p))
     for copy in sent:
         copy.wait_send()
-    put_users.wait()
-    put_items.wait()
+
+
+def write(users, items, out_users, out_items, sem):
+    copies = [
+        pltpu.make_async_copy(users, out_users, sem.at[0]),
+        pltpu.make_async_copy(items, out_items, sem.at[1]),
+    ]
+    for copy in copies:
+        copy.start()
+    for copy in copies:
+        copy.wait()
 
 
 def per_device(rating_tiles, tile_mask, user_rows, item_rows, user_noise, item_noise):
@@ -175,19 +213,18 @@
     half = ib // 2
     bf16, f32 = jnp.bfloat16, jnp.float32
     dma = pltpu.SemaphoreType.DMA
-    return pl.pallas_call(
+    shapes = (
+        jax.ShapeDtypeStruct(user_rows.shape, f32),
+        jax.ShapeDtypeStruct(item_rows.shape, f32),
+    )
+    users, items = pl.pallas_call(
         functools.partial(kernel, lax.axis_size("blk")),
-        out_shape=(
-            jax.ShapeDtypeStruct(user_rows.shape, f32),
-            jax.ShapeDtypeStruct(item_rows.shape, f32),
-        ),
-        in_specs=[pl.BlockSpec(memory_space=pl.ANY)] * 6,
-        out_specs=[pl.BlockSpec(memory_space=pl.ANY)] * 2,
+        out_shape=tuple(pltpu.VMEM(q.shape,q.dtype) for q in shapes),
+        in_specs=[pl.BlockSpec(memory_space=pltpu.HBM)] * 6,
+        out_specs=[pl.BlockSpec(memory_space=pltpu.VMEM)] * 2,
         scratch_shapes=[
             pltpu.VMEM(rating_tiles.shape, bf16),
             pltpu.VMEM(tile_mask.shape, jnp.int32),
-            pltpu.VMEM(user_rows.shape, f32),
-            pltpu.VMEM(item_rows.shape, f32),
             pltpu.VMEM(user_noise.shape, bf16),
             pltpu.VMEM(item_noise.shape, bf16),
             pltpu.VMEM((rounds, n_users, ib), bf16),
@@ -201,14 +238,22 @@
             pltpu.VMEM((ITERS, rounds, rank, half), bf16),
             pltpu.VMEM((ITERS, rounds, rank, half), bf16),
             dma((6,)),
-        ] + [dma((ITERS, rounds))] * 8,
+        ] + [dma((ITERS, rounds, PIECES))] * 2 + [dma((ITERS, rounds))] * 4 + [dma((ITERS, rounds, PIECES))] * 2,
         compiler_params=pltpu.CompilerParams(
-            collective_id=0, has_side_effects=True, vmem_limit_bytes=60 << 20,
+            collective_id=0, has_side_effects=True, vmem_limit_bytes=123 << 19,
         ),
         cost_estimate=pl.CostEstimate(
             flops=ITERS * rounds * 6 * n_users * ib * rank, bytes_accessed=10 << 20, transcendentals=0,
         ),
     )(rating_tiles, tile_mask, user_rows, item_rows, user_noise, item_noise)
+    return pl.pallas_call(
+        write,
+        out_shape=shapes,
+        in_specs=[pl.BlockSpec(memory_space=pl.ANY)] * 2,
+        out_specs=[pl.BlockSpec(memory_space=pltpu.HBM)] * 2,
+        scratch_shapes=[dma((2,))],
+        compiler_params=pltpu.CompilerParams(vmem_limit_bytes=1 << 20),
+    )(users, items)
 
 
 def solution(mesh):

time: 44.1 us -> 37.5 us (0.85)
  local copies, waits for them, and re-layouts: 3.83 us -> 0 us
  Pallas kernels: 39.5 us -> 36.7 us
    unnamed x2 -> x0, local copies, waits for them, and re-layouts: 3.83 us -> none
    pallas_call x1, Pallas kernels: 39.5 us -> 35.7 us  [per_device(): pl.pallas_call(functools.partial(kernel, lax.axis_size('blk')), out_shape...]
    pallas_call x0 -> x1, Pallas kernels: none -> 1.02 us  [per_device(): pl.pallas_call(write, out_shape=shapes, in_specs=[pl.BlockSpec(memory_spa...]
where the time goes in v2:
time: 37.5 us; the launch traced here: 37.3 us
  Pallas kernels  36.7 us (98%)
  between operations  0.64 us (2%)
    pallas_call x1, Pallas kernels, per_device(): pl.pallas_call(functools.partial(kernel, lax.axis_size('blk')), out_shape...  35.7 us
    pallas_call x1, Pallas kernels, per_device(): pl.pallas_call(write, out_shape=shapes, in_specs=[pl.BlockSpec(memory_spa...  1.02 us

profile of v2, /device:TPU:0, one launch (start us, length us, event | category | flops | bytes accessed | tf_op | source)
XLA Modules:
  0.0 37.3 jit_solution(8102935893194155714)
XLA Ops:
  0.6 35.7 %shard_map.77 = (f32[1024,256]{1,0:T(8,128)S(1)}, f32[128,256]{1,0:T(8,128)S(1)}) custom-call(bf16[1024,4,256]{2,1,0:T(4,128)(2,1)} %rating_hbm.1, s32[1024,4,256]{2,1,0:T(4,128)} %mask_hbm.1, f32[1024,256]{1,0:T(8,128)} %users_hbm.1, f32[128,256]{1,0:T(8,128)} %items_hbm.1, bf16[2,1024,256]{2,1,0:T(8,128)(2,1)} %unoise_hbm.1, bf16[2,128,256]{2,1,0:T(8,128)(2,1)} %inoise_hbm.1), custom_call_target="tpu_custom_call" | custom-call | flops 3221225472 | bytes 10485760 | tf_op jit(solution)/shard_map/pallas_call | solution.py:220
  36.3 1.0 %shard_map.78 = (f32[1024,256]{1,0:T(8,128)}, f32[128,256]{1,0:T(8,128)}) custom-call(f32[1024,256]{1,0:T(8,128)S(1)} %get-tuple-element.4.users, f32[128,256]{1,0:T(8,128)S(1)} %get-tuple-element.5.items), custom_call_target="tpu_custom_call" | custom-call | tf_op jit(solution)/shard_map/pallas_call | solution.py:249
